TPU v7x, 32 devices: a whole 2x2x4 slice. The times are simulated.
32 devices in a mesh: groups: 2 (over y), tile: 4 (over z), depth: 2 (over x), gx: 2 (over core).
Axes of the slice: x: 2, y: 2, z: 4, core: 2. Of those that a mesh axis runs over, the one named last changes fastest.
Arguments:
- frame_one: bfloat16 [128, 128, 256], P(('groups', 'depth'), 'tile', 'gx'), parts along dimension 0, may hold values from -6 to 6
- frame_two: bfloat16 [128, 128, 256], P(('groups', 'depth'), 'tile', 'gx'), parts along dimension 0, may hold values from -6 to 6
- shifts: int32 [3, 4, 4, 8], P(None, ('groups', 'depth'), 'tile', 'gx'), parts along dimension 1, may hold values from -1 to 7, as said below
Outputs:
- velocity: float32 [3, 128, 128, 256], P(None, ('groups', 'depth'), 'tile', 'gx'), parts along dimension 1
There are 2 independent parts, one for each index of `groups`. A program takes and returns all parts, laid end to end along the dimension named above; each array names one. Nothing has to cross between parts.
Inputs may be any that keep to these rules, and one draw needn't show every extreme that they name: shifts[0] is -1, 0 or 1; shifts[1] lies in 0 to 3; shifts[2] lies in 0 to 7. The 4 blocks held by one device take their source blocks from exactly 2 distinct tiles of the y axis, 2 blocks from each.
All inputs are finite; a program needn't handle non-finite values.
Results may differ from a plain program's by a relative error of at most 0.0003.
Values may be sent and summed in bfloat16 or wider, within the bound.
A program may use at most 64 MiB of HBM per device.

v0:
```python
import jax
import jax.numpy as jnp
from jax import lax
from jax.sharding import PartitionSpec as P

ITERS = 2


SMOOTH = 1.0


def from_partner(block, axis, apart):
    count = lax.axis_size(axis)
    route = []
    for low in range(count):
        high = low | 1 << apart
        if high != low and high < count:
            route += [(low, high), (high, low)]
    return lax.ppermute(block, axis, route)


def extended(block, sides, width, periodic):
    for axis, dim in sides:
        count = lax.axis_size(axis)
        forward = [(i, i + 1) for i in range(count - 1)]
        if periodic:
            forward.append((count - 1, 0))
        backward = [(target, source) for source, target in forward]
        low = lax.ppermute(
            lax.slice_in_dim(block, block.shape[dim] - width, None, axis=dim), axis, forward
        )
        high = lax.ppermute(lax.slice_in_dim(block, 0, width, axis=dim), axis, backward)
        block = jnp.concatenate([low, block, high], axis=dim)
    return block


def gradients(padded):
    first_frame = padded[0].astype(jnp.float32)
    second_frame = padded[1].astype(jnp.float32)
    bright = 0.5 * (first_frame + second_frame)
    grad_z = 0.5 * (bright[2:, 1:-1, 1:-1] - bright[:-2, 1:-1, 1:-1])
    grad_y = 0.5 * (bright[1:-1, 2:, 1:-1] - bright[1:-1, :-2, 1:-1])
    grad_x = 0.5 * (bright[1:-1, 1:-1, 2:] - bright[1:-1, 1:-1, :-2])
    change = (second_frame - first_frame)[1:-1, 1:-1, 1:-1]
    divisor = SMOOTH + grad_z * grad_z + grad_y * grad_y + grad_x * grad_x
    return (grad_z, grad_y, grad_x, change, divisor)


def sweep(rimmed, coeffs):
    grad_z, grad_y, grad_x, change, divisor = coeffs
    average = (
        rimmed[:, 2:, 1:-1, 1:-1]
        + rimmed[:, :-2, 1:-1, 1:-1]
        + rimmed[:, 1:-1, 2:, 1:-1]
        + rimmed[:, 1:-1, :-2, 1:-1]
        + rimmed[:, 1:-1, 1:-1, 2:]
        + rimmed[:, 1:-1, 1:-1, :-2]
    ) / 6.0
    residual = (grad_z * average[0] + grad_y * average[1] + grad_x * average[2] + change) / divisor
    return jnp.stack(
        [
            average[0] - grad_z * residual,
            average[1] - grad_y * residual,
            average[2] - grad_x * residual,
        ]
    )


def block_sources(routing, first_row, y_blocks, x_total):
    offsets = first_row + jnp.arange(routing.shape[2], dtype=jnp.int32)
    source_row = (offsets[:, None] + routing[1, 0]) % y_blocks
    depth_slot = routing[0, 0] + 1
    x_count = routing.shape[3]
    x_place = (jnp.arange(x_count, dtype=jnp.int32)[None, :] + routing[2, 0]) % x_total
    row_index = depth_slot * x_total + x_place
    return (source_row, row_index)


def block_ranks(source_tile):
    block_count = source_tile.shape[1]
    same_tile = source_tile[:, :, None] == source_tile[:, None, :]
    earlier = jnp.arange(block_count)[None, :] < jnp.arange(block_count)[:, None]
    return jnp.sum(same_tile & earlier[None], axis=2)


def local(frame_one, frame_two, shifts):
    block_edge = frame_two.shape[0]
    x_count = shifts.shape[3]
    x_total = 2 * x_count
    tile_count = lax.axis_size("tile")
    capacity = x_count // min(tile_count, x_count // 2)
    my_tile = lax.axis_index("tile")
    routing = lax.all_gather(shifts, "tile", axis=2, tiled=True)
    wanted_tile, wanted_row = block_sources(routing, 0, tile_count, x_total)
    wanted_rank = block_ranks(wanted_tile)
    slot_ids = jnp.arange(capacity, dtype=jnp.int32)
    matches = (wanted_tile[:, None, :] == my_tile) & (
        wanted_rank[:, None, :] == slot_ids[None, :, None]
    )
    send_rows = jnp.sum(jnp.where(matches, wanted_row[:, None, :], 0), axis=2)
    partner = from_partner(frame_two, "gx", 0)
    full_row = jnp.concatenate([frame_two, partner], axis=2)
    stacked = extended(full_row, (("depth", 0),), block_edge, True)
    flat_rows = send_rows.reshape(-1)

    def cut_block(row_number):
        depth_start = row_number // x_total * block_edge
        x_start = row_number % x_total * block_edge
        return lax.dynamic_slice(
            stacked, (depth_start, 0, x_start), (block_edge, block_edge, block_edge)
        )

    parcel = jax.vmap(cut_block)(flat_rows).reshape(
        tile_count, capacity, block_edge, block_edge, block_edge
    )
    arrived = lax.all_to_all(parcel, "tile", split_axis=0, concat_axis=0, tiled=True)
    arrived = arrived.reshape(tile_count * capacity, block_edge, block_edge, block_edge)
    own_tile, own_row = block_sources(shifts, my_tile, tile_count, x_total)
    own_rank = block_ranks(own_tile)
    pick_rows = (own_tile * capacity + own_rank).reshape(-1)
    fetched = jnp.take(arrived, pick_rows, axis=0)
    fetched = fetched.transpose(1, 2, 0, 3).reshape(frame_two.shape)
    frame_pair = jnp.stack([frame_one, fetched])
    velocity = jnp.zeros((3,) + frame_two.shape, jnp.float32)
    padded = extended(frame_pair, (("tile", 2), ("depth", 1), ("gx", 3)), 1, False)
    coeffs = gradients(padded)
    for sweep_index in range(ITERS):
        rimmed = extended(velocity, (("tile", 2), ("depth", 1), ("gx", 3)), 1, False)
        velocity = sweep(rimmed, coeffs)
    return velocity


def solution(mesh):
    in_specs = (
        P(("groups", "depth"), "tile", "gx"),
        P(("groups", "depth"), "tile", "gx"),
        P(None, ("groups", "depth"), "tile", "gx"),
    )
    out_specs = P(None, ("groups", "depth"), "tile", "gx")
    return jax.shard_map(local, mesh=mesh, in_specs=in_specs, out_specs=out_specs, check_vma=False)
```

profile of v0, /device:TPU:0, one launch (start us, length us, event | category | flops | bytes accessed | tf_op | source)
XLA Modules:
  0.0 191.9 jit_solution(1151490980390607107)
XLA Ops:
  1.3 5.6 %collective-permute-start = (f32[3,32,1,128]{3,2,1,0:T(1,128)S(1)}, f32[3,32,1,128]{3,2,1,0:T(1,128)S(1)}, u32[]{:S(2)}, u32[]{:S(2)}) collective-permute-start(f32[3,32,1,128]{3,2,1,0:T(1,128)S(1)} %broadcast.517), channel_id=1, source_target_pairs={{0,4},{4,8},{8,12},{1,5},{5,9},{9,13},{2,6},{6,10},{10,14},{3,7},{... | collective-permute-start | bytes 147464 | tf_op jit(solution)/shard_map/ppermute | solution.py:29
  7.0 12.7 %all_gather.3 = s32[3,1,4,4]{3,1,0,2:T(1,128)S(1)} all-gather(s32[3,1,1,4]{3,1,0,2:T(1,128)} %bitcast.100), channel_id=1, replica_groups=mesh['groups'=2,'tile'=4,'depth'=2,'gx'=2] {'tile'}, dimensions={2}, use_global_device_ids=true | all-gather | bytes 240 | tf_op jit(solution)/shard_map/all_gather | solution.py:93
  24.2 12.1 %collective-permute-done.8 = bf16[32,32,256]{2,1,0:T(8,128)(2,1)S(1)} collective-permute-done((bf16[32,32,256]{2,1,0:T(8,128)(2,1)S(1)}, bf16[32,32,256]{2,1,0:T(8,128)(2,1)S(1)}, u32[]{:S(2)}, u32[]{:S(2)}) %collective-permute-start.8) | collective-permute-done | bytes 524320 | tf_op jit(solution)/shard_map/ppermute | solution.py:32
  36.3 8.1 %collective-permute-done.7 = bf16[32,32,256]{2,1,0:T(8,128)(2,1)S(1)} collective-permute-done((bf16[32,32,256]{2,1,0:T(8,128)(2,1)S(1)}, bf16[32,32,256]{2,1,0:T(8,128)(2,1)S(1)}, u32[]{:S(2)}, u32[]{:S(2)}) %collective-permute-start.7) | collective-permute-done | bytes 524320 | tf_op jit(solution)/shard_map/ppermute | solution.py:29
  44.5 22.6 %while.1 = (s32[]{:T(128)}, bf16[96,32,256]{2,1,0:T(8,128)(2,1)S(1)}, s32[8,3]{0,1:T(4,128)S(1)}, bf16[8,32,32,32]{3,2,1,0:T(8,128)(2,1)}, s32[]{:T(128)}) while((s32[]{:T(128)}, bf16[96,32,256]{2,1,0:T(8,128)(2,1)S(1)}, s32[8,3]{0,1:T(4,128)S(1)}, bf16[8,32,32,32]{3,2,1,0:T(8,128)(2,1)}, s32[]{:T(128)}) %tuple.40), condition=%wide.while_cond, body=%wide.while_body.sunk | while | flops 2 | bytes 328821 | solution.py:109
  67.1 4.5 %reshape.469 = bf16[4,2,32768]{2,1,0:T(2,128)(2,1)} reshape(bf16[4,2,32,32,32]{4,3,2,1,0:T(8,128)(2,1)} %bitcast.96) | data formatting | bytes 1048576
  71.7 3.5 %all-to-all-start = ((bf16[4,2,32768]{2,1,0:T(2,128)(2,1)}), bf16[4,2,32768]{2,1,0:T(2,128)(2,1)S(1)}, u32[]{:S(2)}, u32[]{:S(2)}) async-start(bf16[4,2,32768]{2,1,0:T(2,128)(2,1)} %reshape.469), calls=%async_computation | async-start | bytes 1048576 | tf_op jit(solution)/shard_map/all_to_all | solution.py:116
  76.2 3.4 %collective-permute-start.3 = (f32[3,1,34,128]{3,2,1,0:T(8,128)}, f32[3,1,34,128]{3,2,1,0:T(8,128)S(1)}, u32[]{:S(2)}, u32[]{:S(2)}) collective-permute-start(f32[3,1,34,128]{3,2,1,0:T(8,128)} %get-tuple-element.42), channel_id=1, source_target_pairs={{0,2},{1,3},{4,6},{5,7},{8,10},{9,11},{12,14},{13,15},{16,18},{17,... | collective-permute-start | bytes 156680 | tf_op jit(solution)/shard_map/ppermute | solution.py:29
  80.9 6.1 %all-to-all-done = bf16[4,2,32768]{2,1,0:T(2,128)(2,1)S(1)} async-done(((bf16[4,2,32768]{2,1,0:T(2,128)(2,1)}), bf16[4,2,32768]{2,1,0:T(2,128)(2,1)S(1)}, u32[]{:S(2)}, u32[]{:S(2)}) %all-to-all-start) | async-done | bytes 524320 | tf_op jit(solution)/shard_map/all_to_all | solution.py:116
  87.0 2.4 %reshape.470 = bf16[4,2,32,32,32]{4,3,2,1,0:T(8,128)(2,1)} reshape(bf16[4,2,32768]{2,1,0:T(2,128)(2,1)S(1)} %all-to-all-done) | data formatting | bytes 1048576
  96.6 3.8 %collective-permute-done.10 = bf16[2,32,1,128]{3,2,1,0:T(2,128)(2,1)S(1)} collective-permute-done((bf16[2,32,1,128]{3,2,1,0:T(2,128)(2,1)S(1)}, bf16[2,32,1,128]{3,2,1,0:T(2,128)(2,1)S(1)}, u32[]{:S(2)}, u32[]{:S(2)}) %collective-permute-start.10) | collective-permute-done | bytes 16416 | tf_op jit(solution)/shard_map/ppermute | solution.py:32
  100.5 3.4 %collective-permute-start.11 = (bf16[2,1,34,128]{3,2,1,0:T(8,128)(2,1)S(1)}, bf16[2,1,34,128]{3,2,1,0:T(8,128)(2,1)S(1)}, u32[]{:S(2)}, u32[]{:S(2)}) collective-permute-start(bf16[2,1,34,128]{3,2,1,0:T(8,128)(2,1)S(1)} %get-tuple-element.50), channel_id=1, source_target_pairs={{0,2},{1,3},{4,6},{5,7},{8,10},{9,11},{12,14},{13,15},{16,18},{17,... | collective-permute-start | bytes 52232 | tf_op jit(solution)/shard_map/ppermute | solution.py:29
  105.2 2.7 %fusion.51 = (f32[3,34,34,1]{3,2,1,0:T(8,128)}, f32[3,34,34,1]{3,2,1,0:T(8,128)}) fusion(f32[3,34,34,128]{3,2,1,0:T(8,128)S(1)} %pad_maximum_fusion), kind=kLoop, calls=%fused_computation.166 | loop fusion | bytes 55488 | tf_op jit(solution)/shard_map/slice | solution.py:32
  114.0 3.0 %collective-permute-start.5 = (f32[3,34,34,1]{2,3,1,0:T(1,128)S(1)}, f32[3,34,34,1]{2,3,1,0:T(1,128)S(1)}, u32[]{:S(2)}, u32[]{:S(2)}) collective-permute-start(f32[3,34,34,1]{2,3,1,0:T(1,128)S(1)} %copy.21), channel_id=1, source_target_pairs={{0,1},{2,3},{4,5},{6,7},{8,9},{10,11},{12,13},{14,15},{16,17},{18,... | collective-permute-start | bytes 41624 | tf_op jit(solution)/shard_map/ppermute | solution.py:29
  128.7 4.2 %collective-permute-start.13 = (bf16[2,34,34,1]{2,0,3,1:T(2,128)(2,1)}, bf16[2,34,34,1]{2,0,3,1:T(2,128)(2,1)}, u32[]{:S(2)}, u32[]{:S(2)}) collective-permute-start(bf16[2,34,34,1]{2,0,3,1:T(2,128)(2,1)} %copy.26), channel_id=1, source_target_pairs={{0,1},{2,3},{4,5},{6,7},{8,9},{10,11},{12,13},{14,15},{16,17},{18,... | collective-permute-start | bytes 13880 | tf_op jit(solution)/shard_map/ppermute | solution.py:29
  132.9 4.8 %fusion.4 = f32[3,32,32,128]{3,2,1,0:T(8,128)S(1)} fusion(f32[3,32,1,128]{3,2,1,0:T(1,128)S(1)} %collective-permute-done.1, f32[3,32,1,128]{3,2,1,0:T(1,128)S(1)} %collective-permute-done, f32[3,34,34,1]{3,2,1,0:T(8,128)} %copy.22, f32[3,1,34,128]{3,2,1,0:T(8,128)} %copy-done.10, f32[3,1,34,128]{3,2,1,0:T(8,128)} %copy-done.9, ...), kind=kLoop, calls=%fused_computation.17 | loop fusion | flops 8650752 | bytes 3376224 | tf_op jit(solution)/shard_map/div | solution.py:51
  141.2 2.4 %pad_maximum_fusion.36 = bf16[2,34,34,130]{3,2,1,0:T(8,128)(2,1)S(1)} fusion(bf16[2,34,34,1]{3,2,1,0:T(8,128)(2,1)} %copy.29, bf16[2,1,34,128]{3,2,1,0:T(8,128)(2,1)} %copy-done.12, bf16[2,32,1,128]{3,2,1,0:T(2,128)(2,1)} %copy-done.8, bf16[1,32,32,128]{3,2,1,0:T(8,128)(2,1)S(1)} %stack_reshape.3, bf16[1,32,32,128]{3,2,1,0:T(8,128)(2,1)S(1)} %bitcast.95, ...), kind=kLoop, calls=%fused_computation.76 | loop fusion | flops 4808960 | bytes 1202240 | tf_op jit(solution)/shard_map/concatenate | solution.py:33
  146.7 3.1 %collective-permute-start.15 = (f32[3,32,1,128]{3,2,1,0:T(1,128)S(1)}, f32[3,32,1,128]{3,2,1,0:T(1,128)S(1)}, u32[]{:S(2)}, u32[]{:S(2)}) collective-permute-start(f32[3,32,1,128]{3,2,1,0:T(1,128)S(1)} %get-tuple-element.44), channel_id=1, source_target_pairs={{0,4},{4,8},{8,12},{1,5},{5,9},{9,13},{2,6},{6,10},{10,14},{3,7},{... | collective-permute-start | bytes 147464 | tf_op jit(solution)/shard_map/ppermute | solution.py:29
  151.5 4.3 %collective-permute-done.16 = f32[3,32,1,128]{3,2,1,0:T(1,128)S(1)} collective-permute-done((f32[3,32,1,128]{3,2,1,0:T(1,128)S(1)}, f32[3,32,1,128]{3,2,1,0:T(1,128)S(1)}, u32[]{:S(2)}, u32[]{:S(2)}) %collective-permute-start.16) | collective-permute-done | bytes 49184 | tf_op jit(solution)/shard_map/ppermute | solution.py:32
  155.8 4.5 %collective-permute-start.18 = (f32[3,1,34,128]{3,2,1,0:T(8,128)S(1)}, f32[3,1,34,128]{3,2,1,0:T(8,128)S(1)}, u32[]{:S(2)}, u32[]{:S(2)}) collective-permute-start(f32[3,1,34,128]{3,2,1,0:T(8,128)S(1)} %get-tuple-element.40), channel_id=1, source_target_pairs={{0,2},{1,3},{4,6},{5,7},{8,10},{9,11},{12,14},{13,15},{16,18},{17,... | collective-permute-start | bytes 156680 | tf_op jit(solution)/shard_map/ppermute | solution.py:29
  162.2 4.3 %collective-permute-done.17 = f32[3,1,34,128]{3,2,1,0:T(8,128)S(1)} collective-permute-done((f32[3,1,34,128]{3,2,1,0:T(8,128)S(1)}, f32[3,1,34,128]{3,2,1,0:T(8,128)S(1)}, u32[]{:S(2)}, u32[]{:S(2)}) %collective-permute-start.17) | collective-permute-done | bytes 52256 | tf_op jit(solution)/shard_map/ppermute | solution.py:32
  166.8 2.6 %fusion.50 = (f32[3,34,34,1]{3,2,1,0:T(8,128)}, f32[3,34,34,1]{3,2,1,0:T(8,128)}) fusion(f32[3,34,34,128]{3,2,1,0:T(8,128)S(1)} %pad_maximum_fusion.1), kind=kLoop, calls=%fused_computation.165 | loop fusion | bytes 55488 | tf_op jit(solution)/shard_map/slice | solution.py:32
  175.5 3.0 %collective-permute-start.20 = (f32[3,34,34,1]{2,3,1,0:T(1,128)S(1)}, f32[3,34,34,1]{2,3,1,0:T(1,128)S(1)}, u32[]{:S(2)}, u32[]{:S(2)}) collective-permute-start(f32[3,34,34,1]{2,3,1,0:T(1,128)S(1)} %copy.32), channel_id=1, source_target_pairs={{0,1},{2,3},{4,5},{6,7},{8,9},{10,11},{12,13},{14,15},{16,17},{18,... | collective-permute-start | bytes 41624 | tf_op jit(solution)/shard_map/ppermute | solution.py:29
  182.9 5.6 %fusion.13 = f32[3,32,32,128]{3,2,1,0:T(8,128)S(1)} fusion(f32[1,32,32,128]{3,2,1,0:T(8,128)S(1)} %get-tuple-element.35, f32[1,32,32,128]{3,2,1,0:T(8,128)S(1)} %get-tuple-element.34, f32[3,34,34,1]{3,2,1,0:T(8,128)} %copy.33, f32[3,1,34,128]{3,2,1,0:T(8,128)S(1)} %collective-permute-done.17, f32[3,1,34,128]{3,2,1,0:T(8,128)S(1)} %collective-permute-done.18, ...), kind=kLoop, calls=%fused_computation.26 | loop fusion | flops 14155776 | bytes 3376224 | tf_op jit(solution)/shard_map/div | solution.py:51
  (133 shorter events, 81.3 us)
Async XLA Ops:
  0.0 75.3 %collective-permute-start.1 = (f32[3,32,1,128]{3,2,1,0:T(1,128)S(1)}, f32[3,32,1,128]{3,2,1,0:T(1,128)S(1)}, u32[]{:S(2)}, u32[]{:S(2)}) collective-permute-start(f32[3,32,1,128]{3,2,1,0:T(1,128)S(1)} %broadcast.517), channel_id=1, source_target_pairs={{4,0},{8,4},{12,8},{5,1},{9,5},{13,9},{6,2},{10,6},{14,10},{7,3},{... | collective-permute-start | bytes 147464 | tf_op jit(solution)/shard_map/ppermute | solution.py:32
  1.3 74.1 %collective-permute-start = (f32[3,32,1,128]{3,2,1,0:T(1,128)S(1)}, f32[3,32,1,128]{3,2,1,0:T(1,128)S(1)}, u32[]{:S(2)}, u32[]{:S(2)}) collective-permute-start(f32[3,32,1,128]{3,2,1,0:T(1,128)S(1)} %broadcast.517), channel_id=1, source_target_pairs={{0,4},{4,8},{8,12},{1,5},{5,9},{9,13},{2,6},{6,10},{10,14},{3,7},{... | collective-permute-start | bytes 147464 | tf_op jit(solution)/shard_map/ppermute | solution.py:29
  6.9 14.4 %collective-permute-start.6 = (bf16[32,32,128]{2,1,0:T(8,128)(2,1)}, bf16[32,32,128]{2,1,0:T(8,128)(2,1)S(1)}, u32[]{:S(2)}, u32[]{:S(2)}) collective-permute-start(bf16[32,32,128]{2,1,0:T(8,128)(2,1)} %param.4), channel_id=1, source_target_pairs={{0,1},{1,0},{2,3},{3,2},{4,5},{5,4},{6,7},{7,6},{8,9},{9,8},{10,11... | collective-permute-start | bytes 786440 | tf_op jit(solution)/shard_map/ppermute | solution.py:19
  21.4 14.9 %collective-permute-start.8 = (bf16[32,32,256]{2,1,0:T(8,128)(2,1)S(1)}, bf16[32,32,256]{2,1,0:T(8,128)(2,1)S(1)}, u32[]{:S(2)}, u32[]{:S(2)}) collective-permute-start(bf16[32,32,256]{2,1,0:T(8,128)(2,1)S(1)} %constant_dynamic-update-slice_fusion), channel_id=1, source_target_pairs={{2,0},{0,2},{3,1},{1,3},{6,4},{4,6},{7,5},{5,7},{10,8},{8,10},{11,... | collective-permute-start | bytes 1572872 | tf_op jit(solution)/shard_map/ppermute | solution.py:32
  22.9 21.5 %collective-permute-start.7 = (bf16[32,32,256]{2,1,0:T(8,128)(2,1)S(1)}, bf16[32,32,256]{2,1,0:T(8,128)(2,1)S(1)}, u32[]{:S(2)}, u32[]{:S(2)}) collective-permute-start(bf16[32,32,256]{2,1,0:T(8,128)(2,1)S(1)} %constant_dynamic-update-slice_fusion), channel_id=1, source_target_pairs={{0,2},{2,0},{1,3},{3,1},{4,6},{6,4},{5,7},{7,5},{8,10},{10,8},{9,1... | collective-permute-start | bytes 1572872 | tf_op jit(solution)/shard_map/ppermute | solution.py:29
  67.1 8.2 %copy-start.13 = (s32[3,1,1,4]{3,2,1,0:T(1,128)S(1)}, s32[3,1,1,4]{3,2,1,0:T(1,128)}, u32[]{:S(2)}) copy-start(s32[3,1,1,4]{3,2,1,0:T(1,128)} %param.5) | copy-start | bytes 148
  71.7 15.3 %all-to-all-start = ((bf16[4,2,32768]{2,1,0:T(2,128)(2,1)}), bf16[4,2,32768]{2,1,0:T(2,128)(2,1)S(1)}, u32[]{:S(2)}, u32[]{:S(2)}) async-start(bf16[4,2,32768]{2,1,0:T(2,128)(2,1)} %reshape.469), calls=%async_computation | async-start | bytes 1048576 | tf_op jit(solution)/shard_map/all_to_all | solution.py:116
  76.2 19.7 %collective-permute-start.3 = (f32[3,1,34,128]{3,2,1,0:T(8,128)}, f32[3,1,34,128]{3,2,1,0:T(8,128)S(1)}, u32[]{:S(2)}, u32[]{:S(2)}) collective-permute-start(f32[3,1,34,128]{3,2,1,0:T(8,128)} %get-tuple-element.42), channel_id=1, source_target_pairs={{0,2},{1,3},{4,6},{5,7},{8,10},{9,11},{12,14},{13,15},{16,18},{17,... | collective-permute-start | bytes 156680 | tf_op jit(solution)/shard_map/ppermute | solution.py:29
  79.6 16.3 %collective-permute-start.2 = (f32[3,1,34,128]{3,2,1,0:T(8,128)S(1)}, f32[3,1,34,128]{3,2,1,0:T(8,128)S(1)}, u32[]{:S(2)}, u32[]{:S(2)}) collective-permute-start(f32[3,1,34,128]{3,2,1,0:T(8,128)S(1)} %get-tuple-element.43), channel_id=1, source_target_pairs={{2,0},{3,1},{6,4},{7,5},{10,8},{11,9},{14,12},{15,13},{18,16},{19,... | collective-permute-start | bytes 156680 | tf_op jit(solution)/shard_map/ppermute | solution.py:32
  93.3 3.3 %collective-permute-start.9 = (bf16[2,32,1,128]{3,2,1,0:T(2,128)(2,1)S(1)}, bf16[2,32,1,128]{3,2,1,0:T(2,128)(2,1)S(1)}, u32[]{:S(2)}, u32[]{:S(2)}) collective-permute-start(bf16[2,32,1,128]{3,2,1,0:T(2,128)(2,1)S(1)} %get-tuple-element.52), channel_id=1, source_target_pairs={{0,4},{4,8},{8,12},{1,5},{5,9},{9,13},{2,6},{6,10},{10,14},{3,7},{... | collective-permute-start | bytes 49160 | tf_op jit(solution)/shard_map/ppermute | solution.py:29
  94.6 5.8 %collective-permute-start.10 = (bf16[2,32,1,128]{3,2,1,0:T(2,128)(2,1)S(1)}, bf16[2,32,1,128]{3,2,1,0:T(2,128)(2,1)S(1)}, u32[]{:S(2)}, u32[]{:S(2)}) collective-permute-start(bf16[2,32,1,128]{3,2,1,0:T(2,128)(2,1)S(1)} %get-tuple-element.53), channel_id=1, source_target_pairs={{4,0},{8,4},{12,8},{5,1},{9,5},{13,9},{6,2},{10,6},{14,10},{7,3},{... | collective-permute-start | bytes 49160 | tf_op jit(solution)/shard_map/ppermute | solution.py:32
  100.4 21.0 %copy-start.8 = (bf16[2,32,1,128]{3,2,1,0:T(2,128)(2,1)}, bf16[2,32,1,128]{3,2,1,0:T(2,128)(2,1)S(1)}, u32[]{:S(2)}) copy-start(bf16[2,32,1,128]{3,2,1,0:T(2,128)(2,1)S(1)} %collective-permute-done.10) | copy-start | bytes 49156
  100.5 21.0 %collective-permute-start.11 = (bf16[2,1,34,128]{3,2,1,0:T(8,128)(2,1)S(1)}, bf16[2,1,34,128]{3,2,1,0:T(8,128)(2,1)S(1)}, u32[]{:S(2)}, u32[]{:S(2)}) collective-permute-start(bf16[2,1,34,128]{3,2,1,0:T(8,128)(2,1)S(1)} %get-tuple-element.50), channel_id=1, source_target_pairs={{0,2},{1,3},{4,6},{5,7},{8,10},{9,11},{12,14},{13,15},{16,18},{17,... | collective-permute-start | bytes 52232 | tf_op jit(solution)/shard_map/ppermute | solution.py:29
  103.9 17.6 %collective-permute-start.12 = (bf16[2,1,34,128]{3,2,1,0:T(8,128)(2,1)S(1)}, bf16[2,1,34,128]{3,2,1,0:T(8,128)(2,1)S(1)}, u32[]{:S(2)}, u32[]{:S(2)}) collective-permute-start(bf16[2,1,34,128]{3,2,1,0:T(8,128)(2,1)S(1)} %get-tuple-element.51), channel_id=1, source_target_pairs={{2,0},{3,1},{6,4},{7,5},{10,8},{11,9},{14,12},{15,13},{18,16},{19,... | collective-permute-start | bytes 52232 | tf_op jit(solution)/shard_map/ppermute | solution.py:32
  110.3 6.7 %collective-permute-start.4 = (f32[3,34,34,1]{2,3,1,0:T(1,128)S(1)}, f32[3,34,34,1]{2,3,1,0:T(1,128)S(1)}, u32[]{:S(2)}, u32[]{:S(2)}) collective-permute-start(f32[3,34,34,1]{2,3,1,0:T(1,128)S(1)} %copy.19), channel_id=1, source_target_pairs={{1,0},{3,2},{5,4},{7,6},{9,8},{11,10},{13,12},{15,14},{17,16},{19,... | collective-permute-start | bytes 41624 | tf_op jit(solution)/shard_map/ppermute | solution.py:32
  114.0 5.3 %collective-permute-start.5 = (f32[3,34,34,1]{2,3,1,0:T(1,128)S(1)}, f32[3,34,34,1]{2,3,1,0:T(1,128)S(1)}, u32[]{:S(2)}, u32[]{:S(2)}) collective-permute-start(f32[3,34,34,1]{2,3,1,0:T(1,128)S(1)} %copy.21), channel_id=1, source_target_pairs={{0,1},{2,3},{4,5},{6,7},{8,9},{10,11},{12,13},{14,15},{16,17},{18,... | collective-permute-start | bytes 41624 | tf_op jit(solution)/shard_map/ppermute | solution.py:29
  127.4 11.7 %collective-permute-start.14 = (bf16[2,34,34,1]{2,0,3,1:T(2,128)(2,1)}, bf16[2,34,34,1]{2,0,3,1:T(2,128)(2,1)}, u32[]{:S(2)}, u32[]{:S(2)}) collective-permute-start(bf16[2,34,34,1]{2,0,3,1:T(2,128)(2,1)} %copy.27), channel_id=1, source_target_pairs={{1,0},{3,2},{5,4},{7,6},{9,8},{11,10},{13,12},{15,14},{17,16},{19,... | collective-permute-start | bytes 13880 | tf_op jit(solution)/shard_map/ppermute | solution.py:32
  128.7 9.0 %collective-permute-start.13 = (bf16[2,34,34,1]{2,0,3,1:T(2,128)(2,1)}, bf16[2,34,34,1]{2,0,3,1:T(2,128)(2,1)}, u32[]{:S(2)}, u32[]{:S(2)}) collective-permute-start(bf16[2,34,34,1]{2,0,3,1:T(2,128)(2,1)} %copy.26), channel_id=1, source_target_pairs={{0,1},{2,3},{4,5},{6,7},{8,9},{10,11},{12,13},{14,15},{16,17},{18,... | collective-permute-start | bytes 13880 | tf_op jit(solution)/shard_map/ppermute | solution.py:29
  146.7 4.8 %collective-permute-start.15 = (f32[3,32,1,128]{3,2,1,0:T(1,128)S(1)}, f32[3,32,1,128]{3,2,1,0:T(1,128)S(1)}, u32[]{:S(2)}, u32[]{:S(2)}) collective-permute-start(f32[3,32,1,128]{3,2,1,0:T(1,128)S(1)} %get-tuple-element.44), channel_id=1, source_target_pairs={{0,4},{4,8},{8,12},{1,5},{5,9},{9,13},{2,6},{6,10},{10,14},{3,7},{... | collective-permute-start | bytes 147464 | tf_op jit(solution)/shard_map/ppermute | solution.py:29
  149.8 6.0 %collective-permute-start.16 = (f32[3,32,1,128]{3,2,1,0:T(1,128)S(1)}, f32[3,32,1,128]{3,2,1,0:T(1,128)S(1)}, u32[]{:S(2)}, u32[]{:S(2)}) collective-permute-start(f32[3,32,1,128]{3,2,1,0:T(1,128)S(1)} %get-tuple-element.45), channel_id=1, source_target_pairs={{4,0},{8,4},{12,8},{5,1},{9,5},{13,9},{6,2},{10,6},{14,10},{7,3},{... | collective-permute-start | bytes 147464 | tf_op jit(solution)/shard_map/ppermute | solution.py:32
  155.8 6.4 %collective-permute-start.18 = (f32[3,1,34,128]{3,2,1,0:T(8,128)S(1)}, f32[3,1,34,128]{3,2,1,0:T(8,128)S(1)}, u32[]{:S(2)}, u32[]{:S(2)}) collective-permute-start(f32[3,1,34,128]{3,2,1,0:T(8,128)S(1)} %get-tuple-element.40), channel_id=1, source_target_pairs={{0,2},{1,3},{4,6},{5,7},{8,10},{9,11},{12,14},{13,15},{16,18},{17,... | collective-permute-start | bytes 156680 | tf_op jit(solution)/shard_map/ppermute | solution.py:29
  160.3 6.1 %collective-permute-start.17 = (f32[3,1,34,128]{3,2,1,0:T(8,128)S(1)}, f32[3,1,34,128]{3,2,1,0:T(8,128)S(1)}, u32[]{:S(2)}, u32[]{:S(2)}) collective-permute-start(f32[3,1,34,128]{3,2,1,0:T(8,128)S(1)} %get-tuple-element.41), channel_id=1, source_target_pairs={{2,0},{3,1},{6,4},{7,5},{10,8},{11,9},{14,12},{15,13},{18,16},{19,... | collective-permute-start | bytes 156680 | tf_op jit(solution)/shard_map/ppermute | solution.py:32
  171.8 6.7 %collective-permute-start.19 = (f32[3,34,34,1]{2,3,1,0:T(1,128)S(1)}, f32[3,34,34,1]{2,3,1,0:T(1,128)S(1)}, u32[]{:S(2)}, u32[]{:S(2)}) collective-permute-start(f32[3,34,34,1]{2,3,1,0:T(1,128)S(1)} %copy.30), channel_id=1, source_target_pairs={{1,0},{3,2},{5,4},{7,6},{9,8},{11,10},{13,12},{15,14},{17,16},{19,... | collective-permute-start | bytes 41624 | tf_op jit(solution)/shard_map/ppermute | solution.py:32
  175.5 5.2 %collective-permute-start.20 = (f32[3,34,34,1]{2,3,1,0:T(1,128)S(1)}, f32[3,34,34,1]{2,3,1,0:T(1,128)S(1)}, u32[]{:S(2)}, u32[]{:S(2)}) collective-permute-start(f32[3,34,34,1]{2,3,1,0:T(1,128)S(1)} %copy.32), channel_id=1, source_target_pairs={{0,1},{2,3},{4,5},{6,7},{8,9},{10,11},{12,13},{14,15},{16,17},{18,... | collective-permute-start | bytes 41624 | tf_op jit(solution)/shard_map/ppermute | solution.py:29
  (12 other events, 27.8 us)
where the time goes:
time: 193 us; the launch traced here: 192 us
  local copies, waits for them, and re-layouts  68.4 us (35%)
  starting transfers between devices  48.8 us (25%)
  waiting for transfers between devices  39.7 us (21%)
  other arithmetic  21.9 us (11%)
  blocking collectives  12.7 us (7%)
    ppermute x10, starting transfers between devices, extended(): lax.ppermute(lax.slice_in_dim(block, block.shape[dim] - width, None, axis...  32.1 us
    ppermute x10, waiting for transfers between devices, extended(): lax.ppermute(lax.slice_in_dim(block, 0, width, axis=dim), axis, backward)  24.5 us
    gather x24, local copies, waits for them, and re-layouts  22.6 us
    ppermute x10, starting transfers between devices, extended(): lax.ppermute(lax.slice_in_dim(block, 0, width, axis=dim), axis, backward)  13.2 us
    all_gather x1, blocking collectives, local(): routing = lax.all_gather(shifts, 'tile', axis=2, tiled=True)  12.7 us
    slice x5, local copies, waits for them, and re-layouts, extended(): lax.slice_in_dim(block, 0, width, axis=dim)  11.3 us
    div x2, other arithmetic, sweep(): (rimmed[:, 2:, 1:-1, 1:-1] + rimmed[:, :-2, 1:-1, 1:-1] + rimmed[:, 1:-1,...  10.5 us
    unnamed x31, local copies, waits for them, and re-layouts  10.2 us
  transfers between devices with their start and end apart: 22, of which 8 were waited for; matrix products, arithmetic and copies ran while one was open for 31% of the time, Pallas kernels for 0%

commit v1 on v0

v1 whole, which is shorter than its diff:
```python
import functools

import jax
import jax.numpy as jnp
from jax import lax
from jax.experimental import pallas as pl
from jax.experimental.pallas import tpu as pltpu
from jax.sharding import PartitionSpec as P

MESH = pl.DeviceIdType.MESH
F32 = jnp.float32
BF16 = jnp.bfloat16
E = 32
L = 128
NB = 4
CAP = 2
PK = 8
PAD = 8
CHUNKS = 2


def regroup(rows, lane):
    a, b, c, d = rows
    low = lane < 64
    r64 = lambda v: pltpu.roll(v, 64, 1)
    a, c = jnp.where(low, a, r64(c)), jnp.where(low, r64(a), c)
    b, d = jnp.where(low, b, r64(d)), jnp.where(low, r64(b), d)
    even = lax.rem(lane, 64) < 32
    a, b = (jnp.where(even, a, pltpu.roll(b, 32, 1)), jnp.where(even, pltpu.roll(a, 96, 1), b))
    c, d = (jnp.where(even, c, pltpu.roll(d, 32, 1)), jnp.where(even, pltpu.roll(c, 96, 1), d))
    return [a, b, c, d]


def kernel(T, Z, f1, f2, sh, out, *scr):
    C = CHUNKS
    S, scr = scr[:C], scr[C:]
    A, scr = scr[:C], scr[C:]
    (B, shr, shs, brp, chs, g, inv, v1p, yb, xb, yv, xv, ybs, xbs, yvs, xvs,
     sem_sh_s, sem_sh_r, sem_loc, sem_gx_s, sem_gx_r, sem_d_s, sem_d_r, sem_f_s, sem_f_r,
     sem_t_s, sem_t_r, sem_h_s, sem_h_r, sem_v_s, sem_v_r) = scr
    CP = PK // C
    m = lax.axis_index("tile")
    z = lax.axis_index("depth")
    x = lax.axis_index("gx")
    px = 1 - x
    nslots = min(Z, 3)
    steps = {1: [], 2: [1]}.get(Z, [1, Z - 1])

    def rcopy(src, dst, ss, rs, dev):
        return pltpu.make_async_remote_copy(
            src_ref=src, dst_ref=dst, send_sem=ss, recv_sem=rs, device_id=dev, device_id_type=MESH)

    barrier = pltpu.get_barrier_semaphore()
    for o in range(1, T):
        pl.semaphore_signal(barrier, inc=1, device_id={"tile": lax.rem(m + o, T)}, device_id_type=MESH)
    for st in steps:
        pl.semaphore_signal(barrier, inc=1, device_id={"depth": lax.rem(z + st, Z)}, device_id_type=MESH)
    pl.semaphore_signal(barrier, inc=1, device_id={"gx": px}, device_id_type=MESH)

    lane = lax.broadcasted_iota(jnp.int32, (E, L), 1)

    for c in range(C):
        def pack(zz, carry, c=c):
            rows = [f2[c * CP + zz + PK * q].astype(F32) for q in range(NB)]
            for b, v in enumerate(regroup(rows, lane)):
                S[c][b, zz] = v.astype(BF16)
            return carry
        lax.fori_loop(0, CP, pack, 0)
    shr[m] = sh[...]

    pl.semaphore_wait(barrier, T - 1 + len(steps) + 1)

    sh_cp = []
    for o in range(1, T):
        t = lax.rem(m + o, T)
        cp = rcopy(sh, shr.at[m], sem_sh_s.at[o], sem_sh_r.at[o], {"tile": t})
        cp.start()
        sh_cp.append(cp)

    gx_cp, d_cp = [], []
    for c in range(C):
        own = S[c].at[pl.ds(0, NB)]
        dl = []
        for k, st in enumerate(steps):
            slot = 1 + (k if Z == 2 else 1 - k)
            cp = rcopy(own, S[c].at[pl.ds(slot * 2 * NB, NB)], sem_d_s.at[c, k], sem_d_r.at[c, k],
                       {"depth": lax.rem(z + st, Z)})
            cp.start()
            dl.append((cp, slot))
        d_cp.append(dl)
    for c in range(C):
        cp = rcopy(S[c].at[pl.ds(0, NB)], S[c].at[pl.ds(NB, NB)], sem_gx_s.at[c], sem_gx_r.at[c], {"gx": px})
        cp.start()
        gx_cp.append(cp)

    for cp in sh_cp:
        cp.wait_recv()
    loc = pltpu.make_async_copy(shr, shs, sem_loc)
    loc.start()
    loc.wait()

    def sources(t):
        tiles = [lax.rem(t + shs[t, 1, b], T) for b in range(NB)]
        ranks = []
        for b in range(NB):
            r = jnp.int32(0)
            for e in range(b):
                r = r + jnp.where(tiles[e] == tiles[b], 1, 0)
            ranks.append(r)
        return tiles, ranks

    def rows_for(t):
        tiles, ranks = sources(t)
        picked = [jnp.int32(0)] * CAP
        for b in range(NB):
            s0 = shs[t, 0, b]
            if Z == 1:
                slot = jnp.int32(0)
            elif Z == 2:
                slot = s0 * s0
            else:
                slot = jnp.where(s0 < 0, 2, s0)
            row = slot * (2 * NB) + lax.rem(b + shs[t, 2, b], 2 * NB)
            for k in range(CAP):
                hit = (tiles[b] == m) & (ranks[b] == k)
                picked[k] = picked[k] + jnp.where(hit, row, 0)
        return picked

    want = [rows_for(lax.rem(m + o, T)) for o in range(T)]

    f_cp = []
    t_cp = []
    for c in range(C):
        gx_cp[c].wait_recv()
        fl = []
        for k, (cp, slot) in enumerate(d_cp[c]):
            cp.wait_recv()
            at = slot * 2 * NB
            f = rcopy(S[c].at[pl.ds(at, NB)], S[c].at[pl.ds(at + NB, NB)],
                      sem_f_s.at[c, k], sem_f_r.at[c, k], {"gx": px})
            f.start()
            fl.append(f)
        for f in fl:
            f.wait_recv()
        f_cp.append(fl)
        tl = []
        for o in list(range(1, T)) + [0]:
            t = lax.rem(m + o, T)
            for k in range(CAP):
                row = want[o][k]

                def cut(zz, carry, c=c, o=o, k=k, row=row):
                    if o == 0:
                        A[c][m * CAP + k, zz] = S[c][row, zz]
                    else:
                        B[c, o, k, zz] = S[c][row, zz]
                    return carry
                lax.fori_loop(0, CP, cut, 0)
            if o:
                cp = rcopy(B.at[c, o], A[c].at[pl.ds(m * CAP, CAP)], sem_t_s.at[c, o], sem_t_r.at[c, o], {"tile": t})
                cp.start()
                tl.append(cp)
        t_cp.append(tl)

    tiles, ranks = sources(m)
    pick = [tiles[b] * CAP + jnp.minimum(ranks[b], CAP - 1) for b in range(NB)]
    src_lane = jnp.where(x == 0, L - 1, 0)
    dst_lane = src_lane
    body = pl.ds(PAD, E)

    xbs[...] = jnp.zeros((E, L), F32)
    for c in range(C):
        for cp in t_cp[c]:
            cp.wait_recv()

        def unpack(zz, carry, c=c):
            rows = [A[c][pick[b], zz].astype(F32) for b in range(NB)]
            for q, w in enumerate(regroup(rows, lane)):
                zi = c * CP + zz + PK * q
                one = f1[zi].astype(F32)
                br = 0.5 * (one + w)
                brp[zi + 1, body] = br
                chs[zi] = w - one
                ybs[0, pl.ds(zi, 1)] = br[0:1]
                ybs[1, pl.ds(zi, 1)] = br[E - 1:E]
                col = pltpu.roll(br, lax.rem(zi - src_lane + L, L), 1)
                xbs[...] = jnp.where(lane == zi, col, xbs[...])
            return carry
        lax.fori_loop(0, CP, unpack, 0)

    def faces(zlo_src, zhi_src, zlo_dst, zhi_dst, ys, yr, xs, xr, ss, rs):
        plan = [
            (ys[1], yr[0], 0, m < T - 1, m > 0, {"tile": jnp.minimum(m + 1, T - 1)}),
            (ys[0], yr[1], 1, m > 0, m < T - 1, {"tile": jnp.maximum(m - 1, 0)}),
            (zhi_src, zlo_dst, 2, z < Z - 1, z > 0, {"depth": jnp.minimum(z + 1, Z - 1)}),
            (zlo_src, zhi_dst, 3, z > 0, z < Z - 1, {"depth": jnp.maximum(z - 1, 0)}),
        ]
        cx = rcopy(xs, xr, ss.at[4], rs.at[4], {"gx": px})
        todo = []
        for src, dst, i, has_to, has_from, dev in plan:
            cp = rcopy(src, dst, ss.at[i], rs.at[i], dev)

            @pl.when(has_to)
            def _():
                cp.start()

            @pl.when(jnp.logical_not(has_from))
            def _():
                dst[...] = jnp.zeros(dst.shape, F32)
            todo.append((cp, has_to, has_from))
        cx.start()

        def wait_recv():
            for cp, has_to, has_from in todo:
                @pl.when(has_from)
                def _():
                    cp.wait_recv()
            cx.wait_recv()

        def wait_send():
            for cp, has_to, has_from in todo:
                @pl.when(has_to)
                def _():
                    cp.wait_send()
            cx.wait_send()
        return wait_recv, wait_send

    wr1, ws1 = faces(brp.at[1, body], brp.at[E, body], brp.at[0, body], brp.at[E + 1, body],
                     [ybs.at[0], ybs.at[1]], [yb.at[0], yb.at[1]], xbs, xb, sem_h_s, sem_h_r)
    wr1()

    is0 = jnp.where(x == 0, 1.0, 0.0).astype(F32)
    is1 = 1.0 - is0

    def x_pair(v, halo):
        nxt = jnp.where(lane == L - 1, halo * is0, pltpu.roll(v, L - 1, 1))
        prv = jnp.where(lane == 0, halo * is1, pltpu.roll(v, 1, 1))
        return nxt, prv

    for i in range(3):
        xvs[i] = jnp.zeros((E, L), F32)

    def first(zi, carry):
        back = lax.rem(dst_lane - zi + L, L)
        brp[zi + 1, pl.ds(PAD - 1, 1)] = yb[0, pl.ds(zi, 1)]
        brp[zi + 1, pl.ds(PAD + E, 1)] = yb[1, pl.ds(zi, 1)]
        br = brp[zi + 1, body]
        gz = 0.5 * (brp[zi + 2, body] - brp[zi, body])
        gy = 0.5 * (brp[zi + 1, pl.ds(PAD + 1, E)] - brp[zi + 1, pl.ds(PAD - 1, E)])
        nxt, prv = x_pair(br, pltpu.roll(xb[...], back, 1))
        gx = 0.5 * (nxt - prv)
        iv = 1.0 / (1.0 + gz * gz + gy * gy + gx * gx)
        res = chs[zi] * iv
        inv[zi] = iv
        move = lax.rem(zi - src_lane + L, L)
        for i, gg in enumerate((gz, gy, gx)):
            g[i, zi] = gg
            v = -gg * res
            v1p[i, zi + 1, body] = v
            yvs[0, i, pl.ds(zi, 1)] = v[0:1]
            yvs[1, i, pl.ds(zi, 1)] = v[E - 1:E]
            xvs[i] = jnp.where(lane == zi, pltpu.roll(v, move, 1), xvs[i])
        return carry
    lax.fori_loop(0, E, first, 0)

    three = pl.ds(0, 3)
    wr2, ws2 = faces(v1p.at[three, 1, body], v1p.at[three, E, body], v1p.at[three, 0, body], v1p.at[three, E + 1, body],
                     [yvs.at[0], yvs.at[1]], [yv.at[0], yv.at[1]], xvs, xv, sem_v_s, sem_v_r)
    wr2()

    def second(zi, carry):
        back = lax.rem(dst_lane - zi + L, L)
        avg = []
        for i in range(3):
            v1p[i, zi + 1, pl.ds(PAD - 1, 1)] = yv[0, i, pl.ds(zi, 1)]
            v1p[i, zi + 1, pl.ds(PAD + E, 1)] = yv[1, i, pl.ds(zi, 1)]
            v = v1p[i, zi + 1, body]
            nxt, prv = x_pair(v, pltpu.roll(xv[i], back, 1))
            total = (v1p[i, zi + 2, body] + v1p[i, zi, body]
                     + v1p[i, zi + 1, pl.ds(PAD + 1, E)] + v1p[i, zi + 1, pl.ds(PAD - 1, E)] + nxt + prv)
            avg.append(total * (1.0 / 6.0))
        gs = [g[i, zi] for i in range(3)]
        res = (gs[0] * avg[0] + gs[1] * avg[1] + gs[2] * avg[2] + chs[zi]) * inv[zi]
        for i in range(3):
            out[i, zi] = avg[i] - gs[i] * res
        return carry
    lax.fori_loop(0, E, second, 0)

    for cp in sh_cp:
        cp.wait_send()
    for c in range(C):
        gx_cp[c].wait_send()
        for cp, slot in d_cp[c]:
            cp.wait_send()
        for cp in f_cp[c]:
            cp.wait_send()
        for cp in t_cp[c]:
            cp.wait_send()
    ws1()
    ws2()


def local(T, Z, frame_one, frame_two, shifts):
    C = CHUNKS
    CP = PK // C
    own = jnp.pad(shifts.reshape(3, NB), ((0, 5), (0, L - NB)))
    nslots = min(Z, 3)
    dma = pltpu.SemaphoreType.DMA
    ns = max(1, nslots - 1)
    vm = pltpu.VMEM
    scratch = [vm((nslots * 2 * NB, CP, E, L), BF16) for _ in range(C)]
    scratch += [vm((T * CAP, CP, E, L), BF16) for _ in range(C)]
    scratch += [
        vm((C, T, CAP, CP, E, L), BF16),
        vm((T, 8, L), jnp.int32),
        pltpu.SMEM((T, 8, L), jnp.int32),
        vm((E + 2, E + 2 * PAD, L), F32),
        vm((E, E, L), F32),
        vm((3, E, E, L), F32),
        vm((E, E, L), F32),
        vm((3, E + 2, E + 2 * PAD, L), F32),
        vm((2, E, L), F32), vm((E, L), F32), vm((2, 3, E, L), F32), vm((3, E, L), F32),
        vm((2, E, L), F32), vm((E, L), F32), vm((2, 3, E, L), F32), vm((3, E, L), F32),
        dma((T,)), dma((T,)), dma, dma((C,)), dma((C,)),
        dma((C, ns)), dma((C, ns)), dma((C, ns)), dma((C, ns)),
        dma((C, T)), dma((C, T)), dma((5,)), dma((5,)), dma((5,)), dma((5,)),
    ]
    return pl.pallas_call(
        functools.partial(kernel, T, Z),
        out_shape=jax.ShapeDtypeStruct((3,) + frame_one.shape, F32),
        in_specs=[pl.BlockSpec(memory_space=pltpu.VMEM)] * 3,
        out_specs=pl.BlockSpec(memory_space=pltpu.VMEM),
        scratch_shapes=scratch,
        compiler_params=pltpu.CompilerParams(
            collective_id=0, has_side_effects=True, vmem_limit_bytes=40 * 1024 * 1024),
        cost_estimate=pl.CostEstimate(flops=131072 * 60, bytes_accessed=2 << 20, transcendentals=0),
        name="warp_flow",
    )(frame_one, frame_two, own)


def solution(mesh):
    spec = P(("groups", "depth"), "tile", "gx")
    vec = P(None, ("groups", "depth"), "tile", "gx")
    body = functools.partial(local, mesh.shape["tile"], mesh.shape["depth"])
    return jax.shard_map(body, mesh=mesh, in_specs=(spec, spec, vec), out_specs=vec, check_vma=False)
```

time: 193 us -> 43.6 us (0.23)
  local copies, waits for them, and re-layouts: 68.4 us -> 3.73 us
  starting transfers between devices: 48.8 us -> 0 us
  waiting for transfers between devices: 39.7 us -> 0 us
  Pallas kernels: 0 us -> 39.6 us
  other arithmetic: 21.9 us -> 0 us
  blocking collectives: 12.7 us -> 0 us
    ppermute x21 -> x0, starting transfers between devices: 45.3 us -> none  [the longest x10 32.1 us: extended(): lax.ppermute(lax.slice_in_dim(block, block.shape[dim] - width, None, axis...]
    pallas_call x0 -> x1, Pallas kernels: none -> 39.6 us  [local(): pl.pallas_call(functools.partial(kernel, T, Z), out_shape=jax.ShapeDtypeS...]
    ppermute x21 -> x0, waiting for transfers between devices: 33.6 us -> none  [the longest x10 24.5 us: extended(): lax.ppermute(lax.slice_in_dim(block, 0, width, axis=dim), axis, backward)]
    gather x25 -> x0, local copies, waits for them, and re-layouts: 24.9 us -> none
    slice x9 -> x0, local copies, waits for them, and re-layouts: 19.4 us -> none  [the longest x5 11.3 us: extended(): lax.slice_in_dim(block, 0, width, axis=dim)]
    all_gather x1 -> x0, blocking collectives: 12.7 us -> none  [local(): routing = lax.all_gather(shifts, 'tile', axis=2, tiled=True)]
    ppermute x6 -> x0, local copies, waits for them, and re-layouts: 12.2 us -> none  [the longest x3 6.51 us: extended(): lax.ppermute(lax.slice_in_dim(block, 0, width, axis=dim), axis, backward)]
    div x2 -> x0, other arithmetic: 10.5 us -> none  [sweep(): (rimmed[:, 2:, 1:-1, 1:-1] + rimmed[:, :-2, 1:-1, 1:-1] + rimmed[:, 1:-1,...]
  transfers between devices with their start and end apart: 22 -> 0, of which waited for: 8 -> 0; matrix products, arithmetic and copies ran while one was open for 31% -> 0% of each run, Pallas kernels for 0% -> 0%
where the time goes in v1:
time: 43.6 us; the launch traced here: 43.4 us
  Pallas kernels  39.6 us (91%)
  local copies, waits for them, and re-layouts  3.73 us (9%)
    pallas_call x1, Pallas kernels, local(): pl.pallas_call(functools.partial(kernel, T, Z), out_shape=jax.ShapeDtypeS...  39.6 us
    unnamed x6, local copies, waits for them, and re-layouts  3.73 us

profile of v1, /device:TPU:0, one launch (start us, length us, event | category | flops | bytes accessed | tf_op | source)
XLA Modules:
  0.0 43.4 jit_solution(5747884316558614704)
XLA Ops:
  0.0 0.7 %copy.6 = s32[3,1,1,4]{3,0,1,2:T(4,128)S(1)} copy(s32[3,1,1,4]{3,2,1,0:T(1,128)} %param.5) | data formatting | bytes 96
  0.7 0.0 copy-start
  0.7 0.9 %copy-done = bf16[32,32,128]{2,1,0:T(8,128)(2,1)S(1)} copy-done((bf16[32,32,128]{2,1,0:T(8,128)(2,1)S(1)}, bf16[32,32,128]{2,1,0:T(8,128)(2,1)}, u32[]{:S(2)}) %copy-start) | copy-done | bytes 262168
  1.6 0.0 copy-start.1
  1.6 0.9 %copy-done.1 = bf16[32,32,128]{2,1,0:T(8,128)(2,1)S(1)} copy-done((bf16[32,32,128]{2,1,0:T(8,128)(2,1)S(1)}, bf16[32,32,128]{2,1,0:T(8,128)(2,1)}, u32[]{:S(2)}) %copy-start.1) | copy-done | bytes 262168
  2.6 39.6 %warp_flow.1 = f32[3,32,32,128]{3,2,1,0:T(8,128)S(1)} custom-call(bf16[32,32,128]{2,1,0:T(8,128)(2,1)S(1)} %copy-done, bf16[32,32,128]{2,1,0:T(8,128)(2,1)S(1)} %copy-done.1, s32[8,128]{1,0:T(8,128)S(1)} %pad.4.sh), custom_call_target="tpu_custom_call" | custom-call | flops 7864320 | bytes 2097152 | tf_op jit(solution)/shard_map/warp_flow/pallas_call | solution.py:328
  42.2 1.1 %copy.8 = f32[3,32,32,128]{3,2,1,0:T(8,128)} copy(f32[3,32,32,128]{3,2,1,0:T(8,128)S(1)} %warp_flow.1) | data formatting | bytes 3145728
  (1 shorter events, 0.0 us)
Async XLA Ops:
  0.7 0.9 %copy-start = (bf16[32,32,128]{2,1,0:T(8,128)(2,1)S(1)}, bf16[32,32,128]{2,1,0:T(8,128)(2,1)}, u32[]{:S(2)}) copy-start(bf16[32,32,128]{2,1,0:T(8,128)(2,1)} %f1.1) | copy-start | bytes 786436
  1.6 0.9 %copy-start.1 = (bf16[32,32,128]{2,1,0:T(8,128)(2,1)S(1)}, bf16[32,32,128]{2,1,0:T(8,128)(2,1)}, u32[]{:S(2)}) copy-start(bf16[32,32,128]{2,1,0:T(8,128)(2,1)} %f2.1) | copy-start | bytes 786436

commit v2 on v1

--- a/solution.py
+++ b/solution.py
@@ -31,13 +31,17 @@
     return [a, b, c, d]
 
 
-def kernel(T, Z, f1, f2, sh, out, *scr):
+def kernel(T, Z, f1_hbm, f2_hbm, sh, out, *scr):
     C = CHUNKS
     S, scr = scr[:C], scr[C:]
     A, scr = scr[:C], scr[C:]
     (B, shr, shs, brp, chs, g, inv, v1p, yb, xb, yv, xv, ybs, xbs, yvs, xvs,
      sem_sh_s, sem_sh_r, sem_loc, sem_gx_s, sem_gx_r, sem_d_s, sem_d_r, sem_f_s, sem_f_r,
-     sem_t_s, sem_t_r, sem_h_s, sem_h_r, sem_v_s, sem_v_r) = scr
+     sem_t_s, sem_t_r, sem_h_s, sem_h_r, sem_v_s, sem_v_r, f1, f2, sem_in) = scr
+    in2 = pltpu.make_async_copy(f2_hbm, f2, sem_in.at[0])
+    in2.start()
+    in1 = pltpu.make_async_copy(f1_hbm, f1, sem_in.at[1])
+    in1.start()
     CP = PK // C
     m = lax.axis_index("tile")
     z = lax.axis_index("depth")
@@ -59,6 +63,7 @@
 
     lane = lax.broadcasted_iota(jnp.int32, (E, L), 1)
 
+    in2.wait()
     for c in range(C):
         def pack(zz, carry, c=c):
             rows = [f2[c * CP + zz + PK * q].astype(F32) for q in range(NB)]
@@ -169,6 +174,7 @@
     body = pl.ds(PAD, E)
 
     xbs[...] = jnp.zeros((E, L), F32)
+    in1.wait()
     for c in range(C):
         for cp in t_cp[c]:
             cp.wait_recv()
@@ -261,7 +267,7 @@
             yvs[1, i, pl.ds(zi, 1)] = v[E - 1:E]
             xvs[i] = jnp.where(lane == zi, pltpu.roll(v, move, 1), xvs[i])
         return carry
-    lax.fori_loop(0, E, first, 0)
+    lax.fori_loop(0, E, first, 0, unroll=4)
 
     three = pl.ds(0, 3)
     wr2, ws2 = faces(v1p.at[three, 1, body], v1p.at[three, E, body], v1p.at[three, 0, body], v1p.at[three, E + 1, body],
@@ -284,7 +290,7 @@
         for i in range(3):
             out[i, zi] = avg[i] - gs[i] * res
         return carry
-    lax.fori_loop(0, E, second, 0)
+    lax.fori_loop(0, E, second, 0, unroll=4)
 
     for cp in sh_cp:
         cp.wait_send()
@@ -324,11 +330,12 @@
         dma((T,)), dma((T,)), dma, dma((C,)), dma((C,)),
         dma((C, ns)), dma((C, ns)), dma((C, ns)), dma((C, ns)),
         dma((C, T)), dma((C, T)), dma((5,)), dma((5,)), dma((5,)), dma((5,)),
+        vm((E, E, L), BF16), vm((E, E, L), BF16), dma((2,)),
     ]
     return pl.pallas_call(
         functools.partial(kernel, T, Z),
         out_shape=jax.ShapeDtypeStruct((3,) + frame_one.shape, F32),
-        in_specs=[pl.BlockSpec(memory_space=pltpu.VMEM)] * 3,
+        in_specs=[pl.BlockSpec(memory_space=pltpu.HBM)] * 2 + [pl.BlockSpec(memory_space=pltpu.VMEM)],
         out_specs=pl.BlockSpec(memory_space=pltpu.VMEM),
         scratch_shapes=scratch,
         compiler_params=pltpu.CompilerParams(

time: 43.6 us -> 37.9 us (0.87)
  Pallas kernels: 39.6 us -> 34 us
    pallas_call x1, Pallas kernels: 39.6 us -> 34 us  [local(): pl.pallas_call(functools.partial(kernel, T, Z), out_shape=jax.ShapeDtypeS...]
where the time goes in v2:
time: 37.9 us; the launch traced here: 37.7 us
  Pallas kernels  34 us (90%)
  local copies, waits for them, and re-layouts  3.73 us (10%)
    pallas_call x1, Pallas kernels, local(): pl.pallas_call(functools.partial(kernel, T, Z), out_shape=jax.ShapeDtypeS...  34 us
    unnamed x6, local copies, waits for them, and re-layouts  3.73 us

profile of v2, /device:TPU:0, one launch (start us, length us, event | category | flops | bytes accessed | tf_op | source)
XLA Modules:
  0.0 37.7 jit_solution(7532970453518635941)
XLA Ops:
  0.0 0.7 %copy.6 = s32[3,1,1,4]{3,0,1,2:T(4,128)S(1)} copy(s32[3,1,1,4]{3,2,1,0:T(1,128)} %param.5) | data formatting | bytes 96
  0.7 0.0 copy-start
  0.7 0.9 %copy-done = bf16[32,32,128]{2,1,0:T(8,128)(2,1)S(1)} copy-done((bf16[32,32,128]{2,1,0:T(8,128)(2,1)S(1)}, bf16[32,32,128]{2,1,0:T(8,128)(2,1)}, u32[]{:S(2)}) %copy-start) | copy-done | bytes 262168
  1.6 0.0 copy-start.1
  1.6 0.9 %copy-done.1 = bf16[32,32,128]{2,1,0:T(8,128)(2,1)S(1)} copy-done((bf16[32,32,128]{2,1,0:T(8,128)(2,1)S(1)}, bf16[32,32,128]{2,1,0:T(8,128)(2,1)}, u32[]{:S(2)}) %copy-start.1) | copy-done | bytes 262168
  2.6 34.0 %warp_flow.1 = f32[3,32,32,128]{3,2,1,0:T(8,128)S(1)} custom-call(bf16[32,32,128]{2,1,0:T(8,128)(2,1)S(1)} %copy-done, bf16[32,32,128]{2,1,0:T(8,128)(2,1)S(1)} %copy-done.1, s32[8,128]{1,0:T(8,128)S(1)} %pad.4.sh), custom_call_target="tpu_custom_call" | custom-call | flops 7864320 | bytes 2097152 | tf_op jit(solution)/shard_map/warp_flow/pallas_call | solution.py:335
  36.6 1.1 %copy.8 = f32[3,32,32,128]{3,2,1,0:T(8,128)} copy(f32[3,32,32,128]{3,2,1,0:T(8,128)S(1)} %warp_flow.1) | data formatting | bytes 3145728
  (1 shorter events, 0.0 us)
Async XLA Ops:
  0.7 0.9 %copy-start = (bf16[32,32,128]{2,1,0:T(8,128)(2,1)S(1)}, bf16[32,32,128]{2,1,0:T(8,128)(2,1)}, u32[]{:S(2)}) copy-start(bf16[32,32,128]{2,1,0:T(8,128)(2,1)} %f1_hbm.1) | copy-start | bytes 786436
  1.6 0.9 %copy-start.1 = (bf16[32,32,128]{2,1,0:T(8,128)(2,1)S(1)}, bf16[32,32,128]{2,1,0:T(8,128)(2,1)}, u32[]{:S(2)}) copy-start(bf16[32,32,128]{2,1,0:T(8,128)(2,1)} %f2_hbm.1) | copy-start | bytes 786436

commit v3 on v2

--- a/solution.py
+++ b/solution.py
@@ -170,41 +170,22 @@
     tiles, ranks = sources(m)
     pick = [tiles[b] * CAP + jnp.minimum(ranks[b], CAP - 1) for b in range(NB)]
     src_lane = jnp.where(x == 0, L - 1, 0)
-    dst_lane = src_lane
     body = pl.ds(PAD, E)
-
-    xbs[...] = jnp.zeros((E, L), F32)
     in1.wait()
-    for c in range(C):
-        for cp in t_cp[c]:
-            cp.wait_recv()
-
-        def unpack(zz, carry, c=c):
-            rows = [A[c][pick[b], zz].astype(F32) for b in range(NB)]
-            for q, w in enumerate(regroup(rows, lane)):
-                zi = c * CP + zz + PK * q
-                one = f1[zi].astype(F32)
-                br = 0.5 * (one + w)
-                brp[zi + 1, body] = br
-                chs[zi] = w - one
-                ybs[0, pl.ds(zi, 1)] = br[0:1]
-                ybs[1, pl.ds(zi, 1)] = br[E - 1:E]
-                col = pltpu.roll(br, lax.rem(zi - src_lane + L, L), 1)
-                xbs[...] = jnp.where(lane == zi, col, xbs[...])
-            return carry
-        lax.fori_loop(0, CP, unpack, 0)
-
-    def faces(zlo_src, zhi_src, zlo_dst, zhi_dst, ys, yr, xs, xr, ss, rs):
+
+    def face_start(c, lo_src, hi_src, lo_dst, hi_dst, ys, yr, xs, xr, ss, rs):
         plan = [
-            (ys[1], yr[0], 0, m < T - 1, m > 0, {"tile": jnp.minimum(m + 1, T - 1)}),
-            (ys[0], yr[1], 1, m > 0, m < T - 1, {"tile": jnp.maximum(m - 1, 0)}),
-            (zhi_src, zlo_dst, 2, z < Z - 1, z > 0, {"depth": jnp.minimum(z + 1, Z - 1)}),
-            (zlo_src, zhi_dst, 3, z > 0, z < Z - 1, {"depth": jnp.maximum(z - 1, 0)}),
+            (ys.at[c, 1], yr.at[c, 0], m < T - 1, m > 0, {"tile": jnp.minimum(m + 1, T - 1)}),
+            (ys.at[c, 0], yr.at[c, 1], m > 0, m < T - 1, {"tile": jnp.maximum(m - 1, 0)}),
         ]
-        cx = rcopy(xs, xr, ss.at[4], rs.at[4], {"gx": px})
+        if c == 0:
+            plan.append((lo_src, hi_dst, z > 0, z < Z - 1, {"depth": jnp.maximum(z - 1, 0)}))
+        if c == C - 1:
+            plan.append((hi_src, lo_dst, z < Z - 1, z > 0, {"depth": jnp.minimum(z + 1, Z - 1)}))
+        cx = rcopy(xs.at[c], xr.at[c], ss.at[c, 4], rs.at[c, 4], {"gx": px})
         todo = []
-        for src, dst, i, has_to, has_from, dev in plan:
-            cp = rcopy(src, dst, ss.at[i], rs.at[i], dev)
+        for i, (src, dst, has_to, has_from, dev) in enumerate(plan):
+            cp = rcopy(src, dst, ss.at[c, i], rs.at[c, i], dev)
 
             @pl.when(has_to)
             def _():
@@ -231,9 +212,30 @@
             cx.wait_send()
         return wait_recv, wait_send
 
-    wr1, ws1 = faces(brp.at[1, body], brp.at[E, body], brp.at[0, body], brp.at[E + 1, body],
-                     [ybs.at[0], ybs.at[1]], [yb.at[0], yb.at[1]], xbs, xb, sem_h_s, sem_h_r)
-    wr1()
+    w_b, w_v = [], []
+    for c in range(C):
+        for cp in t_cp[c]:
+            cp.wait_recv()
+        xbs[c] = jnp.zeros((E, L), F32)
+
+        def unpack(zz, carry, c=c):
+            rows = [A[c][pick[b], zz].astype(F32) for b in range(NB)]
+            acc = xbs[c]
+            for q, w in enumerate(regroup(rows, lane)):
+                zi = c * CP + zz + PK * q
+                pos = zz + CP * q
+                one = f1[zi].astype(F32)
+                br = 0.5 * (one + w)
+                brp[zi + 1, body] = br
+                chs[zi] = w - one
+                ybs[c, 0, pl.ds(pos, 1)] = br[0:1]
+                ybs[c, 1, pl.ds(pos, 1)] = br[E - 1:E]
+                acc = jnp.where(lane == pos, pltpu.roll(br, lax.rem(pos - src_lane + L, L), 1), acc)
+            xbs[c] = acc
+            return carry
+        lax.fori_loop(0, CP, unpack, 0)
+        w_b.append(face_start(c, brp.at[1, body], brp.at[E, body], brp.at[0, body], brp.at[E + 1, body],
+                              ybs, yb, xbs, xb, sem_h_s, sem_h_r))
 
     is0 = jnp.where(x == 0, 1.0, 0.0).astype(F32)
     is1 = 1.0 - is0
@@ -243,54 +245,76 @@
         prv = jnp.where(lane == 0, halo * is1, pltpu.roll(v, 1, 1))
         return nxt, prv
 
-    for i in range(3):
-        xvs[i] = jnp.zeros((E, L), F32)
-
-    def first(zi, carry):
-        back = lax.rem(dst_lane - zi + L, L)
-        brp[zi + 1, pl.ds(PAD - 1, 1)] = yb[0, pl.ds(zi, 1)]
-        brp[zi + 1, pl.ds(PAD + E, 1)] = yb[1, pl.ds(zi, 1)]
-        br = brp[zi + 1, body]
-        gz = 0.5 * (brp[zi + 2, body] - brp[zi, body])
-        gy = 0.5 * (brp[zi + 1, pl.ds(PAD + 1, E)] - brp[zi + 1, pl.ds(PAD - 1, E)])
-        nxt, prv = x_pair(br, pltpu.roll(xb[...], back, 1))
-        gx = 0.5 * (nxt - prv)
-        iv = 1.0 / (1.0 + gz * gz + gy * gy + gx * gx)
-        res = chs[zi] * iv
-        inv[zi] = iv
-        move = lax.rem(zi - src_lane + L, L)
-        for i, gg in enumerate((gz, gy, gx)):
-            g[i, zi] = gg
-            v = -gg * res
-            v1p[i, zi + 1, body] = v
-            yvs[0, i, pl.ds(zi, 1)] = v[0:1]
-            yvs[1, i, pl.ds(zi, 1)] = v[E - 1:E]
-            xvs[i] = jnp.where(lane == zi, pltpu.roll(v, move, 1), xvs[i])
+    def first(q, carry, c):
+        for zz in range(CP):
+            zi, pos = c * CP + zz + PK * q, zz + CP * q
+            brp[zi + 1, pl.ds(PAD - 1, 1)] = yb[c, 0, pl.ds(pos, 1)]
+            brp[zi + 1, pl.ds(PAD + E, 1)] = yb[c, 1, pl.ds(pos, 1)]
+        xh = xb[c]
+        acc = [xvs[c, i] for i in range(3)]
+        for zz in range(CP):
+            zi, pos = c * CP + zz + PK * q, zz + CP * q
+            gz = 0.5 * (brp[zi + 2, body] - brp[zi, body])
+            gy = 0.5 * (brp[zi + 1, pl.ds(PAD + 1, E)] - brp[zi + 1, pl.ds(PAD - 1, E)])
+            nxt, prv = x_pair(brp[zi + 1, body], pltpu.roll(xh, lax.rem(src_lane - pos + L, L), 1))
+            gx = 0.5 * (nxt - prv)
+            iv = 1.0 / (1.0 + gz * gz + gy * gy + gx * gx)
+            res = chs[zi] * iv
+            inv[zi] = iv
+            move = lax.rem(pos - src_lane + L, L)
+            for i, gg in enumerate((gz, gy, gx)):
+                g[i, zi] = gg
+                v = -gg * res
+                v1p[i, zi + 1, body] = v
+                yvs[c, 0, i, pl.ds(pos, 1)] = v[0:1]
+                yvs[c, 1, i, pl.ds(pos, 1)] = v[E - 1:E]
+                acc[i] = jnp.where(lane == pos, pltpu.roll(v, move, 1), acc[i])
+        for i in range(3):
+            xvs[c, i] = acc[i]
         return carry
-    lax.fori_loop(0, E, first, 0, unroll=4)
 
     three = pl.ds(0, 3)
-    wr2, ws2 = faces(v1p.at[three, 1, body], v1p.at[three, E, body], v1p.at[three, 0, body], v1p.at[three, E + 1, body],
-                     [yvs.at[0], yvs.at[1]], [yv.at[0], yv.at[1]], xvs, xv, sem_v_s, sem_v_r)
-    wr2()
-
-    def second(zi, carry):
-        back = lax.rem(dst_lane - zi + L, L)
-        avg = []
-        for i in range(3):
-            v1p[i, zi + 1, pl.ds(PAD - 1, 1)] = yv[0, i, pl.ds(zi, 1)]
-            v1p[i, zi + 1, pl.ds(PAD + E, 1)] = yv[1, i, pl.ds(zi, 1)]
-            v = v1p[i, zi + 1, body]
-            nxt, prv = x_pair(v, pltpu.roll(xv[i], back, 1))
-            total = (v1p[i, zi + 2, body] + v1p[i, zi, body]
-                     + v1p[i, zi + 1, pl.ds(PAD + 1, E)] + v1p[i, zi + 1, pl.ds(PAD - 1, E)] + nxt + prv)
-            avg.append(total * (1.0 / 6.0))
-        gs = [g[i, zi] for i in range(3)]
-        res = (gs[0] * avg[0] + gs[1] * avg[1] + gs[2] * avg[2] + chs[zi]) * inv[zi]
-        for i in range(3):
-            out[i, zi] = avg[i] - gs[i] * res
+    xvs[...] = jnp.zeros(xvs.shape, F32)
+    for c in range(C):
+        if c == 0:
+            w_b[c][0]()
+            lax.fori_loop(1, NB, functools.partial(first, c=c), 0)
+            for later in range(1, C):
+                w_b[later][0]()
+            lax.fori_loop(0, 1, functools.partial(first, c=c), 0)
+        else:
+            lax.fori_loop(0, NB, functools.partial(first, c=c), 0)
+        w_v.append(face_start(c, v1p.at[three, 1, body], v1p.at[three, E, body], v1p.at[three, 0, body],
+                              v1p.at[three, E + 1, body], yvs, yv, xvs, xv, sem_v_s, sem_v_r))
+
+    def second(q, carry, c):
+        for zz in range(CP):
+            zi, pos = c * CP + zz + PK * q, zz + CP * q
+            for i in range(3):
+                v1p[i, zi + 1, pl.ds(PAD - 1, 1)] = yv[c, 0, i, pl.ds(pos, 1)]
+                v1p[i, zi + 1, pl.ds(PAD + E, 1)] = yv[c, 1, i, pl.ds(pos, 1)]
+        for zz in range(CP):
+            zi, pos = c * CP + zz + PK * q, zz + CP * q
+            back = lax.rem(src_lane - pos + L, L)
+            avg = []
+            for i in range(3):
+                nxt, prv = x_pair(v1p[i, zi + 1, body], pltpu.roll(xv[c, i], back, 1))
+                total = (v1p[i, zi + 2, body] + v1p[i, zi, body]
+                         + v1p[i, zi + 1, pl.ds(PAD + 1, E)] + v1p[i, zi + 1, pl.ds(PAD - 1, E)] + nxt + prv)
+                avg.append(total * (1.0 / 6.0))
+            gs = [g[i, zi] for i in range(3)]
+            res = (gs[0] * avg[0] + gs[1] * avg[1] + gs[2] * avg[2] + chs[zi]) * inv[zi]
+            for i in range(3):
+                out[i, zi] = avg[i] - gs[i] * res
         return carry
-    lax.fori_loop(0, E, second, 0, unroll=4)
+
+    w_v[0][0]()
+    lax.fori_loop(1, NB, functools.partial(second, c=0), 0)
+    for c in range(1, C):
+        w_v[c][0]()
+    lax.fori_loop(0, 1, functools.partial(second, c=0), 0)
+    for c in range(1, C):
+        lax.fori_loop(0, NB, functools.partial(second, c=c), 0)
 
     for cp in sh_cp:
         cp.wait_send()
@@ -302,8 +326,9 @@
             cp.wait_send()
         for cp in t_cp[c]:
             cp.wait_send()
-    ws1()
-    ws2()
+    for c in range(C):
+        w_b[c][1]()
+        w_v[c][1]()
 
 
 def local(T, Z, frame_one, frame_two, shifts):
@@ -325,11 +350,11 @@
         vm((3, E, E, L), F32),
         vm((E, E, L), F32),
         vm((3, E + 2, E + 2 * PAD, L), F32),
-        vm((2, E, L), F32), vm((E, L), F32), vm((2, 3, E, L), F32), vm((3, E, L), F32),
-        vm((2, E, L), F32), vm((E, L), F32), vm((2, 3, E, L), F32), vm((3, E, L), F32),
+        vm((C, 2, E // C, L), F32), vm((C, E, L), F32), vm((C, 2, 3, E // C, L), F32), vm((C, 3, E, L), F32),
+        vm((C, 2, E // C, L), F32), vm((C, E, L), F32), vm((C, 2, 3, E // C, L), F32), vm((C, 3, E, L), F32),
         dma((T,)), dma((T,)), dma, dma((C,)), dma((C,)),
         dma((C, ns)), dma((C, ns)), dma((C, ns)), dma((C, ns)),
-        dma((C, T)), dma((C, T)), dma((5,)), dma((5,)), dma((5,)), dma((5,)),
+        dma((C, T)), dma((C, T)), dma((C, 5)), dma((C, 5)), dma((C, 5)), dma((C, 5)),
         vm((E, E, L), BF16), vm((E, E, L), BF16), dma((2,)),
     ]
     return pl.pallas_call(

time: 37.9 us -> 36.5 us (0.963)
  Pallas kernels: 34 us -> 32.5 us
    pallas_call x1, Pallas kernels: 34 us -> 32.5 us  [local(): pl.pallas_call(functools.partial(kernel, T, Z), out_shape=jax.ShapeDtypeS...]
where the time goes in v3:
time: 36.5 us; the launch traced here: 36.3 us
  Pallas kernels  32.5 us (89%)
  local copies, waits for them, and re-layouts  3.73 us (10%)
    pallas_call x1, Pallas kernels, local(): pl.pallas_call(functools.partial(kernel, T, Z), out_shape=jax.ShapeDtypeS...  32.5 us
    unnamed x6, local copies, waits for them, and re-layouts  3.73 us

profile of v3, /device:TPU:0, one launch (start us, length us, event | category | flops | bytes accessed | tf_op | source)
XLA Modules:
  0.0 36.3 jit_solution(13867554045960856691)
XLA Ops:
  0.0 0.7 %copy.6 = s32[3,1,1,4]{3,0,1,2:T(4,128)S(1)} copy(s32[3,1,1,4]{3,2,1,0:T(1,128)} %param.5) | data formatting | bytes 96
  0.7 0.0 copy-start
  0.7 0.9 %copy-done = bf16[32,32,128]{2,1,0:T(8,128)(2,1)S(1)} copy-done((bf16[32,32,128]{2,1,0:T(8,128)(2,1)S(1)}, bf16[32,32,128]{2,1,0:T(8,128)(2,1)}, u32[]{:S(2)}) %copy-start) | copy-done | bytes 262168
  1.6 0.0 copy-start.1
  1.6 0.9 %copy-done.1 = bf16[32,32,128]{2,1,0:T(8,128)(2,1)S(1)} copy-done((bf16[32,32,128]{2,1,0:T(8,128)(2,1)S(1)}, bf16[32,32,128]{2,1,0:T(8,128)(2,1)}, u32[]{:S(2)}) %copy-start.1) | copy-done | bytes 262168
  2.6 32.5 %warp_flow.1 = f32[3,32,32,128]{3,2,1,0:T(8,128)S(1)} custom-call(bf16[32,32,128]{2,1,0:T(8,128)(2,1)S(1)} %copy-done, bf16[32,32,128]{2,1,0:T(8,128)(2,1)S(1)} %copy-done.1, s32[8,128]{1,0:T(8,128)S(1)} %pad.4.sh), custom_call_target="tpu_custom_call" | custom-call | flops 7864320 | bytes 2097152 | tf_op jit(solution)/shard_map/warp_flow/pallas_call | solution.py:360
  35.1 1.1 %copy.8 = f32[3,32,32,128]{3,2,1,0:T(8,128)} copy(f32[3,32,32,128]{3,2,1,0:T(8,128)S(1)} %warp_flow.1) | data formatting | bytes 3145728
  (1 shorter events, 0.0 us)
Async XLA Ops:
  0.7 0.9 %copy-start = (bf16[32,32,128]{2,1,0:T(8,128)(2,1)S(1)}, bf16[32,32,128]{2,1,0:T(8,128)(2,1)}, u32[]{:S(2)}) copy-start(bf16[32,32,128]{2,1,0:T(8,128)(2,1)} %f1_hbm.1) | copy-start | bytes 786436
  1.6 0.9 %copy-start.1 = (bf16[32,32,128]{2,1,0:T(8,128)(2,1)S(1)}, bf16[32,32,128]{2,1,0:T(8,128)(2,1)}, u32[]{:S(2)}) copy-start(bf16[32,32,128]{2,1,0:T(8,128)(2,1)} %f2_hbm.1) | copy-start | bytes 786436

commit v4 on v3

--- a/solution.py
+++ b/solution.py
@@ -16,7 +16,8 @@
 CAP = 2
 PK = 8
 PAD = 8
-CHUNKS = 2
+CHUNKS = 4
+FACE_CHUNKS = 2
 
 
 def regroup(rows, lane):
@@ -31,18 +32,16 @@
     return [a, b, c, d]
 
 
-def kernel(T, Z, f1_hbm, f2_hbm, sh, out, *scr):
+def kernel(T, Z, f1, f2, sh, out, *scr):
     C = CHUNKS
     S, scr = scr[:C], scr[C:]
     A, scr = scr[:C], scr[C:]
     (B, shr, shs, brp, chs, g, inv, v1p, yb, xb, yv, xv, ybs, xbs, yvs, xvs,
      sem_sh_s, sem_sh_r, sem_loc, sem_gx_s, sem_gx_r, sem_d_s, sem_d_r, sem_f_s, sem_f_r,
-     sem_t_s, sem_t_r, sem_h_s, sem_h_r, sem_v_s, sem_v_r, f1, f2, sem_in) = scr
-    in2 = pltpu.make_async_copy(f2_hbm, f2, sem_in.at[0])
-    in2.start()
-    in1 = pltpu.make_async_copy(f1_hbm, f1, sem_in.at[1])
-    in1.start()
+     sem_t_s, sem_t_r, sem_h_s, sem_h_r, sem_v_s, sem_v_r) = scr
     CP = PK // C
+    H = FACE_CHUNKS
+    FP = PK // H
     m = lax.axis_index("tile")
     z = lax.axis_index("depth")
     x = lax.axis_index("gx")
@@ -63,14 +62,13 @@
 
     lane = lax.broadcasted_iota(jnp.int32, (E, L), 1)
 
-    in2.wait()
     for c in range(C):
         def pack(zz, carry, c=c):
             rows = [f2[c * CP + zz + PK * q].astype(F32) for q in range(NB)]
             for b, v in enumerate(regroup(rows, lane)):
                 S[c][b, zz] = v.astype(BF16)
             return carry
-        lax.fori_loop(0, CP, pack, 0)
+        lax.fori_loop(0, CP, pack, 0, unroll=True)
     shr[m] = sh[...]
 
     pl.semaphore_wait(barrier, T - 1 + len(steps) + 1)
@@ -149,7 +147,7 @@
             f.wait_recv()
         f_cp.append(fl)
         tl = []
-        for o in list(range(1, T)) + [0]:
+        for o in [T // 2] + [o for o in range(1, T) if o != T // 2] + [0]:
             t = lax.rem(m + o, T)
             for k in range(CAP):
                 row = want[o][k]
@@ -160,7 +158,7 @@
                     else:
                         B[c, o, k, zz] = S[c][row, zz]
                     return carry
-                lax.fori_loop(0, CP, cut, 0)
+                lax.fori_loop(0, CP, cut, 0, unroll=True)
             if o:
                 cp = rcopy(B.at[c, o], A[c].at[pl.ds(m * CAP, CAP)], sem_t_s.at[c, o], sem_t_r.at[c, o], {"tile": t})
                 cp.start()
@@ -171,7 +169,6 @@
     pick = [tiles[b] * CAP + jnp.minimum(ranks[b], CAP - 1) for b in range(NB)]
     src_lane = jnp.where(x == 0, L - 1, 0)
     body = pl.ds(PAD, E)
-    in1.wait()
 
     def face_start(c, lo_src, hi_src, lo_dst, hi_dst, ys, yr, xs, xr, ss, rs):
         plan = [
@@ -180,7 +177,7 @@
         ]
         if c == 0:
             plan.append((lo_src, hi_dst, z > 0, z < Z - 1, {"depth": jnp.maximum(z - 1, 0)}))
-        if c == C - 1:
+        if c == H - 1:
             plan.append((hi_src, lo_dst, z < Z - 1, z > 0, {"depth": jnp.minimum(z + 1, Z - 1)}))
         cx = rcopy(xs.at[c], xr.at[c], ss.at[c, 4], rs.at[c, 4], {"gx": px})
         todo = []
@@ -213,28 +210,29 @@
         return wait_recv, wait_send
 
     w_b, w_v = [], []
-    for c in range(C):
-        for cp in t_cp[c]:
-            cp.wait_recv()
-        xbs[c] = jnp.zeros((E, L), F32)
-
-        def unpack(zz, carry, c=c):
-            rows = [A[c][pick[b], zz].astype(F32) for b in range(NB)]
-            acc = xbs[c]
-            for q, w in enumerate(regroup(rows, lane)):
-                zi = c * CP + zz + PK * q
-                pos = zz + CP * q
-                one = f1[zi].astype(F32)
-                br = 0.5 * (one + w)
-                brp[zi + 1, body] = br
-                chs[zi] = w - one
-                ybs[c, 0, pl.ds(pos, 1)] = br[0:1]
-                ybs[c, 1, pl.ds(pos, 1)] = br[E - 1:E]
-                acc = jnp.where(lane == pos, pltpu.roll(br, lax.rem(pos - src_lane + L, L), 1), acc)
-            xbs[c] = acc
-            return carry
-        lax.fori_loop(0, CP, unpack, 0)
-        w_b.append(face_start(c, brp.at[1, body], brp.at[E, body], brp.at[0, body], brp.at[E + 1, body],
+    for h in range(H):
+        xbs[h] = jnp.zeros((E, L), F32)
+        for c in range(h * C // H, (h + 1) * C // H):
+            for cp in t_cp[c]:
+                cp.wait_recv()
+
+            def unpack(zz, carry, c=c, h=h):
+                rows = [A[c][pick[b], zz].astype(F32) for b in range(NB)]
+                acc = xbs[h]
+                for q, w in enumerate(regroup(rows, lane)):
+                    zi = c * CP + zz + PK * q
+                    pos = c * CP - h * FP + zz + FP * q
+                    one = f1[zi].astype(F32)
+                    br = 0.5 * (one + w)
+                    brp[zi + 1, body] = br
+                    chs[zi] = w - one
+                    ybs[h, 0, pl.ds(pos, 1)] = br[0:1]
+                    ybs[h, 1, pl.ds(pos, 1)] = br[E - 1:E]
+                    acc = jnp.where(lane == pos, pltpu.roll(br, lax.rem(pos - src_lane + L, L), 1), acc)
+                xbs[h] = acc
+                return carry
+            lax.fori_loop(0, CP, unpack, 0, unroll=True)
+        w_b.append(face_start(h, brp.at[1, body], brp.at[E, body], brp.at[0, body], brp.at[E + 1, body],
                               ybs, yb, xbs, xb, sem_h_s, sem_h_r))
 
     is0 = jnp.where(x == 0, 1.0, 0.0).astype(F32)
@@ -246,14 +244,14 @@
         return nxt, prv
 
     def first(q, carry, c):
-        for zz in range(CP):
-            zi, pos = c * CP + zz + PK * q, zz + CP * q
+        for zz in range(FP):
+            zi, pos = c * FP + zz + PK * q, zz + FP * q
             brp[zi + 1, pl.ds(PAD - 1, 1)] = yb[c, 0, pl.ds(pos, 1)]
             brp[zi + 1, pl.ds(PAD + E, 1)] = yb[c, 1, pl.ds(pos, 1)]
         xh = xb[c]
         acc = [xvs[c, i] for i in range(3)]
-        for zz in range(CP):
-            zi, pos = c * CP + zz + PK * q, zz + CP * q
+        for zz in range(FP):
+            zi, pos = c * FP + zz + PK * q, zz + FP * q
             gz = 0.5 * (brp[zi + 2, body] - brp[zi, body])
             gy = 0.5 * (brp[zi + 1, pl.ds(PAD + 1, E)] - brp[zi + 1, pl.ds(PAD - 1, E)])
             nxt, prv = x_pair(brp[zi + 1, body], pltpu.roll(xh, lax.rem(src_lane - pos + L, L), 1))
@@ -275,11 +273,11 @@
 
     three = pl.ds(0, 3)
     xvs[...] = jnp.zeros(xvs.shape, F32)
-    for c in range(C):
+    for c in range(H):
         if c == 0:
             w_b[c][0]()
             lax.fori_loop(1, NB, functools.partial(first, c=c), 0)
-            for later in range(1, C):
+            for later in range(1, H):
                 w_b[later][0]()
             lax.fori_loop(0, 1, functools.partial(first, c=c), 0)
         else:
@@ -288,13 +286,13 @@
                               v1p.at[three, E + 1, body], yvs, yv, xvs, xv, sem_v_s, sem_v_r))
 
     def second(q, carry, c):
-        for zz in range(CP):
-            zi, pos = c * CP + zz + PK * q, zz + CP * q
+        for zz in range(FP):
+            zi, pos = c * FP + zz + PK * q, zz + FP * q
             for i in range(3):
                 v1p[i, zi + 1, pl.ds(PAD - 1, 1)] = yv[c, 0, i, pl.ds(pos, 1)]
                 v1p[i, zi + 1, pl.ds(PAD + E, 1)] = yv[c, 1, i, pl.ds(pos, 1)]
-        for zz in range(CP):
-            zi, pos = c * CP + zz + PK * q, zz + CP * q
+        for zz in range(FP):
+            zi, pos = c * FP + zz + PK * q, zz + FP * q
             back = lax.rem(src_lane - pos + L, L)
             avg = []
             for i in range(3):
@@ -310,10 +308,10 @@
 
     w_v[0][0]()
     lax.fori_loop(1, NB, functools.partial(second, c=0), 0)
-    for c in range(1, C):
+    for c in range(1, H):
         w_v[c][0]()
     lax.fori_loop(0, 1, functools.partial(second, c=0), 0)
-    for c in range(1, C):
+    for c in range(1, H):
         lax.fori_loop(0, NB, functools.partial(second, c=c), 0)
 
     for cp in sh_cp:
@@ -326,13 +324,13 @@
             cp.wait_send()
         for cp in t_cp[c]:
             cp.wait_send()
-    for c in range(C):
-        w_b[c][1]()
-        w_v[c][1]()
+    for h in range(H):
+        w_b[h][1]()
+        w_v[h][1]()
 
 
 def local(T, Z, frame_one, frame_two, shifts):
-    C = CHUNKS
+    C, H = CHUNKS, FACE_CHUNKS
     CP = PK // C
     own = jnp.pad(shifts.reshape(3, NB), ((0, 5), (0, L - NB)))
     nslots = min(Z, 3)
@@ -350,17 +348,17 @@
         vm((3, E, E, L), F32),
         vm((E, E, L), F32),
         vm((3, E + 2, E + 2 * PAD, L), F32),
-        vm((C, 2, E // C, L), F32), vm((C, E, L), F32), vm((C, 2, 3, E // C, L), F32), vm((C, 3, E, L), F32),
-        vm((C, 2, E // C, L), F32), vm((C, E, L), F32), vm((C, 2, 3, E // C, L), F32), vm((C, 3, E, L), F32),
+        vm((H, 2, E // H, L), F32), vm((H, E, L), F32), vm((H, 2, 3, E // H, L), F32), vm((H, 3, E, L), F32),
+        vm((H, 2, E // H, L), F32), vm((H, E, L), F32), vm((H, 2, 3, E // H, L), F32), vm((H, 3, E, L), F32),
         dma((T,)), dma((T,)), dma, dma((C,)), dma((C,)),
         dma((C, ns)), dma((C, ns)), dma((C, ns)), dma((C, ns)),
-        dma((C, T)), dma((C, T)), dma((C, 5)), dma((C, 5)), dma((C, 5)), dma((C, 5)),
-        vm((E, E, L), BF16), vm((E, E, L), BF16), dma((2,)),
+        dma((C, T)), dma((C, T)), dma((H, 5)), dma((H, 5)), dma((H, 5)), dma((H, 5)),
+
     ]
     return pl.pallas_call(
         functools.partial(kernel, T, Z),
         out_shape=jax.ShapeDtypeStruct((3,) + frame_one.shape, F32),
-        in_specs=[pl.BlockSpec(memory_space=pltpu.HBM)] * 2 + [pl.BlockSpec(memory_space=pltpu.VMEM)],
+        in_specs=[pl.BlockSpec(memory_space=pltpu.VMEM)] * 3,
         out_specs=pl.BlockSpec(memory_space=pltpu.VMEM),
         scratch_shapes=scratch,
         compiler_params=pltpu.CompilerParams(

time: 36.5 us -> 36.1 us (0.989)
  Pallas kernels: 32.5 us -> 32.1 us
    pallas_call x1, Pallas kernels: 32.5 us -> 32.1 us  [local(): pl.pallas_call(functools.partial(kernel, T, Z), out_shape=jax.ShapeDtypeS...]
where the time goes in v4:
time: 36.1 us; the launch traced here: 35.9 us
  Pallas kernels  32.1 us (89%)
  local copies, waits for them, and re-layouts  3.73 us (10%)
    pallas_call x1, Pallas kernels, local(): pl.pallas_call(functools.partial(kernel, T, Z), out_shape=jax.ShapeDtypeS...  32.1 us
    unnamed x6, local copies, waits for them, and re-layouts  3.73 us

profile of v4, /device:TPU:0, one launch (start us, length us, event | category | flops | bytes accessed | tf_op | source)
XLA Modules:
  0.0 35.9 jit_solution(13409093236071644384)
XLA Ops:
  0.0 0.7 %copy.6 = s32[3,1,1,4]{3,0,1,2:T(4,128)S(1)} copy(s32[3,1,1,4]{3,2,1,0:T(1,128)} %param.5) | data formatting | bytes 96
  0.7 0.0 copy-start
  0.7 0.9 %copy-done = bf16[32,32,128]{2,1,0:T(8,128)(2,1)S(1)} copy-done((bf16[32,32,128]{2,1,0:T(8,128)(2,1)S(1)}, bf16[32,32,128]{2,1,0:T(8,128)(2,1)}, u32[]{:S(2)}) %copy-start) | copy-done | bytes 262168
  1.6 0.0 copy-start.1
  1.6 0.9 %copy-done.1 = bf16[32,32,128]{2,1,0:T(8,128)(2,1)S(1)} copy-done((bf16[32,32,128]{2,1,0:T(8,128)(2,1)S(1)}, bf16[32,32,128]{2,1,0:T(8,128)(2,1)}, u32[]{:S(2)}) %copy-start.1) | copy-done | bytes 262168
  2.6 32.1 %warp_flow.1 = f32[3,32,32,128]{3,2,1,0:T(8,128)S(1)} custom-call(bf16[32,32,128]{2,1,0:T(8,128)(2,1)S(1)} %copy-done, bf16[32,32,128]{2,1,0:T(8,128)(2,1)S(1)} %copy-done.1, s32[8,128]{1,0:T(8,128)S(1)} %pad.4.sh), custom_call_target="tpu_custom_call" | custom-call | flops 7864320 | bytes 2097152 | tf_op jit(solution)/shard_map/warp_flow/pallas_call | solution.py:358
  34.7 1.1 %copy.8 = f32[3,32,32,128]{3,2,1,0:T(8,128)} copy(f32[3,32,32,128]{3,2,1,0:T(8,128)S(1)} %warp_flow.1) | data formatting | bytes 3145728
  (1 shorter events, 0.0 us)
Async XLA Ops:
  0.7 0.9 %copy-start = (bf16[32,32,128]{2,1,0:T(8,128)(2,1)S(1)}, bf16[32,32,128]{2,1,0:T(8,128)(2,1)}, u32[]{:S(2)}) copy-start(bf16[32,32,128]{2,1,0:T(8,128)(2,1)} %f1.1) | copy-start | bytes 786436
  1.6 0.9 %copy-start.1 = (bf16[32,32,128]{2,1,0:T(8,128)(2,1)S(1)}, bf16[32,32,128]{2,1,0:T(8,128)(2,1)}, u32[]{:S(2)}) copy-start(bf16[32,32,128]{2,1,0:T(8,128)(2,1)} %f2.1) | copy-start | bytes 786436
